TPU v7x, 256 devices: a whole 4x4x8 slice. The times are simulated.
256 devices in a mesh: ch: 128 (over x, z, y), src: 2 (over core).
Axes of the slice: x: 4, y: 4, z: 8, core: 2. Of those that a mesh axis runs over, the one named last changes fastest.
Arguments:
- spectra: float32 [8192, 2, 2048], P('ch'), may hold values from -6 to 6
- source_ids: int32 [256], replicated, may hold values from 0 to 8191
- offset_bins: int32 [8192, 256], P('ch', 'src'), may hold values from 0 to 959
- owner_slots: int32 [1024], replicated, may hold values from 0 to 1023, each once
Outputs:
- stacks: float32 [1024, 128], P(('ch', 'src'))
All inputs are finite; a program needn't handle non-finite values.
Results may differ from a plain program's by a relative error of at most 0.0037.
Values sent between devices are 32-bit elements; how exact they have to be, the bound alone decides.
No kernel may reach another device: no remote copies, remote signals or barrier semaphores. Data moves between devices by JAX's collectives and lax.ppermute only.
A program may use at most 64 MiB of HBM per device.

v0:
```python
import functools

import jax
import jax.numpy as jnp
import numpy as np
from jax import lax
from jax.experimental import pallas as pl
from jax.experimental.pallas import tpu as pltpu
from jax.sharding import Mesh
from jax.sharding import PartitionSpec as P

LAGS = 128
CLASSES = 16
FFT = 256
WIDTH = 128
HALF = FFT // 2
PARTS = 4 * CLASSES
W_STEP = PARTS + 8
P_STEP = FFT + 8
X, Z, Y = 4, 8, 4
PLANE = ("x", "y")
CHIPS = ("x", "z", "y")
ROUNDS = 2
highest = lax.Precision.HIGHEST


def tables(bins):
    q = np.arange(WIDTH)
    f = np.arange(FFT)
    low = f[:HALF]
    minus = (-low) % FFT
    spread = np.zeros((CLASSES, 4, HALF, 2, WIDTH))
    gain = np.zeros((CLASSES, 4, HALF))
    for p in range(CLASSES):
        k = CLASSES * q + p
        d = np.exp(2j * np.pi * (np.outer(k, q) % bins) / bins) @ np.exp(-2j * np.pi * (np.outer(q, f) % FFT) / FFT)
        plus, back = d[:, :HALF].T.copy(), d[:, minus].T.conj().copy()
        spread[p, 0, :, 0], spread[p, 0, :, 1] = plus.real, -plus.imag
        spread[p, 1, :, 0], spread[p, 1, :, 1] = plus.imag, plus.real
        spread[p, 2, :, 0], spread[p, 2, :, 1] = back.real, back.imag
        spread[p, 3, :, 0], spread[p, 3, :, 1] = back.imag, -back.real
        last = d[:, HALF]
        spread[p, 2, 0, 0], spread[p, 2, 0, 1] = last.real, -last.imag
        spread[p, 3, 0, 0], spread[p, 3, 0, 1] = last.imag, last.real
        odd = low % 2 == 1
        gain[p] = np.where(odd, np.sin(np.pi * p / 16), np.cos(np.pi * p / 16))
        gain[p, 2:] *= np.where(odd, -1.0, 1.0)
    j = np.arange(LAGS)
    angle = 2 * np.pi * (np.outer(low, j) % FFT) / FFT
    c, s = 2 * np.cos(angle) / FFT, 2 * np.sin(angle) / FFT
    odd = (low % 2 == 1)[:, None]
    back = np.stack([np.where(odd, s, c), np.where(odd, c, -s)])
    back[0, 0] = 2 / FFT
    back[1, 0] = 2 * np.where(j % 2 == 1, -1.0, 1.0) / FFT
    back = back.reshape(FFT, LAGS) * (CLASSES * bins ** -1.5)
    gain = gain.transpose(2, 1, 0)
    weights = np.stack([gain, gain * np.array([1.0, -1.0, 1.0, -1.0])[:, None]])
    weights[0, 0, 2:] = 0
    weights[1, 0, :2], weights[1, 0, 2:] = 0, gain[0, 2:]
    weights = np.pad(weights.reshape(2, HALF, PARTS), ((0, 0), (0, 0), (0, 128 - PARTS)))
    return spread.reshape(CLASSES, 4 * HALF, 2 * WIDTH), weights, back


def high_low(values):
    high = np.asarray(values, np.float32).astype(jnp.bfloat16)
    low = (np.asarray(values, np.float32) - high.astype(np.float32)).astype(jnp.bfloat16)
    return jnp.asarray(high), jnp.asarray(low)


def by_class(rows):
    count, two, bins = rows.shape
    return rows.reshape(count, 2, WIDTH, CLASSES).transpose(0, 3, 1, 2)


def nt(a, b):
    return lax.dot_general(a, b, (((1,), (1,)), ((), ())), preferred_element_type=jnp.float32)


def split_here(values):
    high = values.astype(jnp.bfloat16)
    return high, (values - high.astype(jnp.float32)).astype(jnp.bfloat16)


def stack_kernel(z_ref, th_ref, tl_ref, a_ref, bins_ref, slot_ref, bh_ref, bl_ref, out_ref, w_ref, p_ref, acc_ref):
    local = bins_ref.shape[0]

    for p in range(CLASSES):
        zh, zl = split_here(z_ref[:, p * 2 * WIDTH : (p + 1) * 2 * WIDTH])
        u = nt(th_ref[p], zh) + nt(tl_ref[p], zh) + nt(th_ref[p], zl)
        for c in range(4):
            w_ref[pl.ds(c * CLASSES + p, HALF, stride=W_STEP), :] = u[c * HALF : (c + 1) * HALF]

    @pl.loop(0, HALF, unroll=16)
    def _(f):
        w = w_ref[pl.ds(pl.multiple_of(f * W_STEP, 8), PARTS), :].astype(jnp.bfloat16)
        o = jnp.dot(a_ref[f], jnp.concatenate([w, w], axis=0), preferred_element_type=jnp.float32)
        p_ref[pl.ds(f, local, stride=P_STEP), :] = o[:local]
        p_ref[pl.ds(f + HALF, local, stride=P_STEP), :] = o[local:]

    acc_ref[...] = jnp.zeros_like(acc_ref)
    group = 8

    @pl.loop(0, local // group)
    def _(g):
        member, prod = [], []
        for i in range(group):
            r = g * group + i
            mine = slot_ref[...] == bins_ref[pl.ds(r, 1), :]
            member.append(jnp.where(mine, 1.0, 0.0).astype(jnp.bfloat16))
            prod.append(p_ref[pl.ds(pl.multiple_of(r * P_STEP, 8), FFT), :].astype(jnp.bfloat16))
        acc_ref[...] += nt(jnp.concatenate(member, axis=1), jnp.concatenate(prod, axis=1))

    ah, al = split_here(acc_ref[...])
    out_ref[...] = (
        jnp.dot(ah, bh_ref[...], preferred_element_type=jnp.float32)
        + jnp.dot(al, bh_ref[...], preferred_element_type=jnp.float32)
        + jnp.dot(ah, bl_ref[...], preferred_element_type=jnp.float32)
    )


def stacked(sources, spread_h, spread_l, receivers, bins, bin_of, back_h, back_l):
    local = bins.shape[0]
    slots = bin_of.shape[0]
    vmem = pl.BlockSpec(memory_space=pltpu.VMEM)
    return pl.pallas_call(
        stack_kernel,
        out_shape=jax.ShapeDtypeStruct((slots, LAGS), jnp.float32),
        in_specs=[vmem] * 8,
        out_specs=vmem,
        scratch_shapes=[
            pltpu.VMEM((HALF * W_STEP, 128), jnp.float32),
            pltpu.VMEM((local * P_STEP, 128), jnp.float32),
            pltpu.VMEM((slots, FFT), jnp.float32),
        ],
        compiler_params=pltpu.CompilerParams(vmem_limit_bytes=48 * 1024 * 1024),
        cost_estimate=pl.CostEstimate(flops=9 * 10**9, bytes_accessed=16 * 2**20, transcendentals=0),
    )(sources, spread_h, spread_l, receivers, bins, bin_of, back_h, back_l)


def receiver_kernel(z_ref, th_ref, tl_ref, gain_ref, out_ref, t_ref, v_ref):
    local = z_ref.shape[0]
    block = 2 * WIDTH

    @pl.loop(0, t_ref.shape[0] // block)
    def _(i):
        at = pl.multiple_of(i * block, block)
        t_ref[pl.ds(at, block), :local] = z_ref[:, pl.ds(at, block)].T

    odd = lax.broadcasted_iota(jnp.int32, (2 * WIDTH, local), 0) % 2 == 1
    bins = t_ref.shape[0] // 2
    for p in range(CLASSES):
        z = jnp.concatenate([t_ref[pl.ds(i * bins + p, WIDTH, stride=CLASSES), :][:, :local] for i in range(2)], axis=0)
        zh, zl = split_here(jnp.where(odd, -z, z))
        u = (
            jnp.dot(th_ref[p], zh, preferred_element_type=jnp.float32)
            + jnp.dot(tl_ref[p], zh, preferred_element_type=jnp.float32)
            + jnp.dot(th_ref[p], zl, preferred_element_type=jnp.float32)
        )
        for c in range(4):
            v_ref[pl.ds(c * CLASSES + p, HALF, stride=W_STEP), :local] = u[c * HALF : (c + 1) * HALF]

    def place(f, swap):
        v = v_ref[pl.ds(pl.multiple_of(f * W_STEP, 8), PARTS), :local]
        a, b, c, d = (v[i * CLASSES : (i + 1) * CLASSES] for i in range(4))
        w = jnp.concatenate([b, a, d, c], axis=0) if swap else v
        real = v.T * gain_ref[0, pl.ds(f, 1), :PARTS]
        imag = w.T * gain_ref[1, pl.ds(f, 1), :PARTS]
        high, low = split_here(jnp.concatenate([real, imag], axis=0))
        out_ref[f] = jnp.concatenate([high, low], axis=1)

    @pl.loop(0, HALF, unroll=8)
    def _(f):
        place(f, True)

    place(0, False)


def receiver_side(flat, spread_h, spread_l, gain):
    local, width = flat.shape
    vmem = pl.BlockSpec(memory_space=pltpu.VMEM)
    return pl.pallas_call(
        receiver_kernel,
        out_shape=jax.ShapeDtypeStruct((HALF, 2 * local, 2 * PARTS), jnp.bfloat16),
        in_specs=[vmem] * 4,
        out_specs=vmem,
        scratch_shapes=[pltpu.VMEM((width, 128), jnp.float32), pltpu.VMEM((HALF * W_STEP, 128), jnp.float32)],
        compiler_params=pltpu.CompilerParams(vmem_limit_bytes=40 * 1024 * 1024),
        cost_estimate=pl.CostEstimate(flops=6 * 10**9, bytes_accessed=14 * 2**20, transcendentals=0),
    )(flat, spread_h, spread_l, gain)


def where_of(ids, local):
    chip = ids // local
    return chip, (chip // Y) % Z, (chip // (Z * Y)) * Y + chip % Y


def fits(ids, local):
    chip, plane, _ = where_of(ids, local)
    per_chip = jnp.sum((chip[:, None] == chip[None, :]).astype(jnp.int32), axis=1)
    per_plane = jnp.sum((plane[:, None] == plane[None, :]).astype(jnp.int32), axis=1)
    return (jnp.max(per_chip) <= X * Y) & (jnp.max(per_plane) <= ROUNDS * X * Y)


def select_rows(table, rows):
    return jnp.dot(table.astype(jnp.float32), rows, precision=highest, preferred_element_type=jnp.float32)


def bin_counts(bins, slots, owner_slots):
    flat = bins.reshape(1, -1)
    digit = lax.broadcasted_iota(jnp.int32, (32, 1), 0)
    high = (flat // 32 == digit).astype(jnp.bfloat16)
    low = (flat % 32 == digit).astype(jnp.bfloat16)
    per_bin = nt(high, low).reshape(1, slots)
    at = lax.broadcasted_iota(jnp.int32, (slots, 1), 0) == owner_slots[None, :]
    return jnp.sum(jnp.where(at, per_bin, 0.0), axis=1)


def per_device(spectra, source_ids, offset_bins, owner_slots):
    local, two, bins = spectra.shape
    count = offset_bins.shape[1]
    slots = owner_slots.shape[0]
    spots = X * Y
    rows = count // spots
    spread, gain, back = tables(bins)
    spread_h, spread_l = high_low(spread)
    back_h, back_l = high_low(back)
    src_rank = lax.axis_index("core")
    ch_rank = lax.axis_index(CHIPS)
    my_plane = lax.axis_index("z")
    my_spot = lax.axis_index(PLANE)
    mine = lax.dynamic_slice_in_dim(source_ids, src_rank * count, count, 0)
    chip, plane, spot = where_of(mine, local)
    key = (plane * spots + spot) * count + lax.iota(jnp.int32, count)
    rank = jnp.sum((key[None, :] < key[:, None]).astype(jnp.int32), axis=1)
    dest = rank % spots
    flat = spectra.reshape(local, 2 * bins)

    row = lax.broadcasted_iota(jnp.int32, (spots, 1), 0)
    owned = jnp.where(chip == ch_rank, mine % local, -1)
    channel = jnp.max(jnp.where(dest[None, :] == row, owned[None, :], -1), axis=1)
    picked = select_rows(channel[:, None] == lax.broadcasted_iota(jnp.int32, (1, local), 1), flat)
    picked = by_class(picked.reshape(spots, 2, bins)).reshape(spots, 2 * bins)
    came = lax.all_to_all(picked, PLANE, 0, 0, tiled=True)

    before = jnp.sum((plane[None, :] < lax.broadcasted_iota(jnp.int32, (Z, 1), 0)).astype(jnp.int32), axis=1)
    first = before + (my_spot - before) % spots
    turn = (rank - first[plane]) // spots
    here = (plane == my_plane) & (dest == my_spot)
    at = here[None, :] & (turn[None, :] == lax.broadcasted_iota(jnp.int32, (ROUNDS, 1), 0))
    sender = jnp.max(jnp.where(at, spot[None, :], -1), axis=1)
    kept = select_rows(sender[:, None] == lax.broadcasted_iota(jnp.int32, (1, spots), 1), came)
    wide = jnp.broadcast_to(kept[None], (Z,) + kept.shape)
    came = lax.all_to_all(wide, "z", 0, 0, tiled=True).reshape(Z * ROUNDS, 2 * bins)

    at = rank[None, :] == lax.broadcasted_iota(jnp.int32, (rows, 1), 0) * spots + my_spot
    sender = jnp.max(jnp.where(at, (plane * ROUNDS + turn)[None, :], -1), axis=1)
    kept = select_rows(sender[:, None] == lax.broadcasted_iota(jnp.int32, (1, Z * ROUNDS), 1), came)
    kept, later = lax.optimization_barrier((kept, flat))
    wide = jnp.broadcast_to(kept[None], (spots,) + kept.shape)
    routed = lax.all_to_all(wide, PLANE, 0, 0, tiled=True).reshape(count, 2 * bins)
    receivers = receiver_side(later, spread_h, spread_l, jnp.asarray(gain, jnp.float32))

    place = dest * rows + rank // spots
    placing = place[:, None] == lax.broadcasted_iota(jnp.int32, (count, count), 1)

    def summed():
        ids = jnp.sum(jnp.where(placing, mine[:, None], 0), axis=0)
        chan_ids = ch_rank * local + lax.broadcasted_iota(jnp.int32, (1, local), 1)
        found = select_rows(ids[:, None] == chan_ids, flat)
        home = jnp.sum(lax.all_to_all(found, CHIPS, 0, 0, tiled=True), axis=0, keepdims=True)
        home = by_class(home.reshape(1, 2, bins)).reshape(1, 2 * bins)
        return lax.all_to_all(jnp.broadcast_to(home, (count, 2 * bins)), CHIPS, 0, 0, tiled=True)

    ok = fits(source_ids[:count], local) & fits(source_ids[count:], local)
    sources = lax.cond(ok, lambda: routed, summed)

    iota = lax.broadcasted_iota(jnp.int32, (slots, 1), 0)
    bin_of = jnp.sum(jnp.where(iota == owner_slots[None, :], lax.broadcasted_iota(jnp.int32, (1, slots), 1), 0), axis=1)
    bins_here = select_rows(offset_bins, placing.astype(jnp.float32)).astype(jnp.int32)
    counts = bin_counts(offset_bins, slots, owner_slots)
    bin_wide = jnp.broadcast_to(bin_of[:, None], (slots, 128))
    panel = stacked(sources, spread_h, spread_l, receivers, bins_here, bin_wide, back_h, back_l)

    devices = X * Y * Z
    own = slots // (2 * devices)
    packed = jnp.concatenate(
        [panel.reshape(devices, 2, own * LAGS), jnp.pad(counts.reshape(devices, 2, own), ((0, 0), (0, 0), (0, LAGS - own)))],
        axis=2,
    )
    here = lax.dynamic_index_in_dim(packed, src_rank, 1, keepdims=False)
    there = lax.dynamic_index_in_dim(packed, 1 - src_rank, 1, keepdims=False)
    halves = here + lax.ppermute(there, "core", [(0, 1), (1, 0)])
    total = jnp.sum(lax.all_to_all(halves, CHIPS, 0, 0, tiled=True), axis=0)
    stack_sum = total[: own * LAGS].reshape(own, LAGS)
    stack_count = total[own * LAGS : own * LAGS + own]
    return stack_sum / jnp.sqrt(jnp.maximum(stack_count, 1.0))[:, None]


def solution(mesh):
    fine = Mesh(mesh.devices.reshape(X, Z, Y, 2), ("x", "z", "y", "core"))
    placed = (P(CHIPS, None, None), P(), P(CHIPS, "core"), P())
    return jax.shard_map(
        per_device, mesh=fine, in_specs=placed, out_specs=P(CHIPS + ("core",), None), check_vma=False
    )
```

profile of v0, /device:TPU:1, one launch (start us, length us, event | category | flops | bytes accessed | tf_op | source)
XLA Modules:
  0.0 124.1 jit_solution(15129407960969096552)
XLA Ops:
  0.0 0.9 compare_select_fusion.17
  1.1 1.8 %copy.32 = f32[8,8,2,2048]{3,1,2,0:T(8,128)S(1)} copy(f32[8,8,2,2048]{3,2,1,0:T(2,128)} %bitcast.74) | data formatting | bytes 2097152
  3.7 1.7 %fusion.5 = f32[16,16,2,128]{3,0,1,2:T(8,128)S(1)} fusion(f32[2,128,16,64]{3,2,1,0:T(8,128)S(1)} %bitcast.72, s32[16]{0:T(128)S(1)} %select_reduce_fusion.3), kind=kOutput, calls=%fused_computation.13 | convolution fusion | flops 50332672 | bytes 1310784 | tf_op jit(solution)/shard_map/dot_general | solution.py:205
  5.3 0.9 copy.25
  6.2 7.6 %all-to-all-start.2 = ((f32[16,1,4096]{2,1,0:T(1,128)}), f32[16,1,4096]{2,1,0:T(1,128)S(1)}, u32[]{:S(2)}, u32[]{:S(2)}) async-start(f32[16,1,4096]{2,1,0:T(1,128)} %bitcast.17), calls=%async_computation.2 | async-start | bytes 524288 | tf_op jit(solution)/shard_map/all_to_all | solution.py:243
  14.6 5.0 %multiply_add_fusion = (s32[128]{0:T(128)S(1)}, s32[128]{0:T(128)S(1)}, s32[128]{0:T(128)S(1)}) fusion(s32[128]{0:T(128)S(1)} %get-tuple-element.35, s32[128]{0:T(128)S(1)} %convert_reduce_fusion, s32[]{:T(128)} %bitcast.11, s32[]{:T(128)} %bitcast.10, s32[]{:T(128)} %bitcast.9, s32[]{:T(128)} %bitcast.8, s32[]{:T(128)} %bitcast.7, s32[]{:T(128)} %bitcast.6, ...), kind=kLoop, calls=%fused_computation.129 | loop fusion | flops 6656 | bytes 3104 | tf_op jit(solution)/shard_map/add | solution.py:256
  19.8 1.5 %all-to-all-done.2 = f32[16,1,4096]{2,1,0:T(1,128)S(1)} async-done(((f32[16,1,4096]{2,1,0:T(1,128)}), f32[16,1,4096]{2,1,0:T(1,128)S(1)}, u32[]{:S(2)}, u32[]{:S(2)}) %all-to-all-start.2) | async-done | bytes 262176 | tf_op jit(solution)/shard_map/all_to_all | solution.py:243
  21.6 0.8 broadcast_in_dim.141
  22.4 8.2 %all-to-all-start.3 = ((f32[8,2,4096]{2,1,0:T(2,128)}), f32[8,2,4096]{2,1,0:T(2,128)S(1)}, u32[]{:S(2)}, u32[]{:S(2)}) async-start(f32[8,2,4096]{2,1,0:T(2,128)} %broadcast_in_dim.141), calls=%async_computation.3 | async-start | bytes 524288 | tf_op jit(solution)/shard_map/all_to_all | solution.py:253
  33.0 7.1 %all-to-all-done.3 = f32[8,2,4096]{2,1,0:T(2,128)S(1)} async-done(((f32[8,2,4096]{2,1,0:T(2,128)}), f32[8,2,4096]{2,1,0:T(2,128)S(1)}, u32[]{:S(2)}, u32[]{:S(2)}) %all-to-all-start.3) | async-done | bytes 262176 | tf_op jit(solution)/shard_map/all_to_all | solution.py:253
  40.5 1.5 %broadcast_in_dim.142 = f32[16,8,4096]{2,1,0:T(8,128)} broadcast(f32[8,4096]{1,0:T(8,128)S(1)} %fusion.23), dimensions={1,2} | broadcast | bytes 2228224 | tf_op jit(solution)/shard_map/broadcast_in_dim | solution.py:259
  42.1 5.9 %all-to-all-start.4 = ((f32[16,8,4096]{2,1,0:T(8,128)}), f32[16,8,4096]{2,1,0:T(8,128)S(1)}, u32[]{:S(2)}, u32[]{:S(2)}) async-start(f32[16,8,4096]{2,1,0:T(8,128)} %broadcast_in_dim.142), calls=%async_computation.4 | async-start | bytes 4194304 | tf_op jit(solution)/shard_map/all_to_all | solution.py:260
  53.8 2.2 %copy-done = bf16[16,512,256]{2,1,0:T(8,128)(2,1)S(1)} copy-done((bf16[16,512,256]{2,1,0:T(8,128)(2,1)S(1)}, bf16[16,512,256]{2,1,0:T(8,128)(2,1)}, u32[]{:S(2)}) %copy-start) | copy-done | bytes 4194328
  56.0 2.2 %copy-done.2 = bf16[16,512,256]{2,1,0:T(8,128)(2,1)S(1)} copy-done((bf16[16,512,256]{2,1,0:T(8,128)(2,1)S(1)}, bf16[16,512,256]{2,1,0:T(8,128)(2,1)}, u32[]{:S(2)}) %copy-start.2) | copy-done | bytes 4194328
  58.2 9.9 %shard_map.91.a_ref = bf16[128,128,128]{2,1,0:T(8,128)(2,1)S(1)} custom-call(f32[64,4096]{1,0:T(8,128)S(1)} %bitcast.70, bf16[16,512,256]{2,1,0:T(8,128)(2,1)S(1)} %copy-done, bf16[16,512,256]{2,1,0:T(8,128)(2,1)S(1)} %copy-done.2, f32[2,128,128]{2,1,0:T(8,128)S(1)} %copy-done.3), custom_call_target="tpu_custom_call" | custom-call | flops 6000000000 | bytes 14680064 | tf_op jit(solution)/shard_map/pallas_call | solution.py:181
  68.1 1.9 %copy-done.6 = bf16[128,128,128]{2,1,0:T(8,128)(2,1)} copy-done((bf16[128,128,128]{2,1,0:T(8,128)(2,1)}, bf16[128,128,128]{2,1,0:T(8,128)(2,1)S(1)}, u32[]{:S(2)}) %copy-start.6) | copy-done | bytes 4194328
  70.0 3.3 %all-to-all-done.4 = f32[16,8,4096]{2,1,0:T(8,128)S(1)} async-done(((f32[16,8,4096]{2,1,0:T(8,128)}), f32[16,8,4096]{2,1,0:T(8,128)S(1)}, u32[]{:S(2)}, u32[]{:S(2)}) %all-to-all-start.4) | async-done | bytes 2097184 | tf_op jit(solution)/shard_map/all_to_all | solution.py:260
  73.3 1.3 %conditional.1 = (f32[128,4096]{1,0:T(8,128)}) conditional(s32[]{:T(128)} %convert_element_type.42, (s32[128]{0:T(128)S(1)}, pred[128,128]{1,0:T(8,128)(4,1)S(1)}, s32[]{:T(128)}, f32[64,4096]{1,0:T(8,128)S(1)}) %tuple.41, f32[16,8,4096]{2,1,0:T(8,128)S(1)} %all-to-all-done.4), branch_computations={%region_13.16_spmd, %region_16.17_spmd} | conditional | flops 403214272 | bytes 24234012 | solution.py:275
  73.3 1.3 %copy.47 = f32[128,4096]{1,0:T(8,128)} copy(f32[128,4096]{1,0:T(8,128)S(1)} %bitcast.73) | data formatting | bytes 4194304 | tf_op jit(solution)/shard_map/cond
  74.9 2.2 %copy-done.1 = bf16[16,512,256]{2,1,0:T(8,128)(2,1)S(1)} copy-done((bf16[16,512,256]{2,1,0:T(8,128)(2,1)S(1)}, bf16[16,512,256]{2,1,0:T(8,128)(2,1)}, u32[]{:S(2)}) %copy-start.1) | copy-done | bytes 4194328
  77.0 16.9 %shard_map.92 = f32[1024,128]{1,0:T(8,128)S(1)} custom-call(f32[128,4096]{1,0:T(8,128)} %get-tuple-element.62.z_ref, bf16[16,512,256]{2,1,0:T(8,128)(2,1)S(1)} %copy-done.1, bf16[16,512,256]{2,1,0:T(8,128)(2,1)} %constant.228.clone.tl_ref, bf16[128,128,128]{2,1,0:T(8,128)(2,1)} %copy-done.6, s32[64,128]{1,0:T(8,128)S(1)} %fusion.8.bins_ref, ...), custom_call_target="tpu_custom_call" | custom-call | flops 8999999488 | bytes 16777216 | tf_op jit(solution)/shard_map/pallas_call | solution.py:125
  95.2 5.7 %collective-permute-start = (f32[128,640]{1,0:T(8,128)S(1)}, f32[128,640]{1,0:T(8,128)S(1)}, u32[]{:S(2)}, u32[]{:S(2)}) collective-permute-start(f32[128,640]{1,0:T(8,128)S(1)} %bitcast.76), channel_id=1, source_target_pairs={{0,1},{1,0},{2,3},{3,2},{4,5},{5,4},{6,7},{7,6},{8,9},{9,8},{10,11... | collective-permute-start | bytes 983048 | tf_op jit(solution)/shard_map/ppermute | solution.py:292
  100.8 1.3 %collective-permute-done = f32[128,640]{1,0:T(8,128)S(1)} collective-permute-done((f32[128,640]{1,0:T(8,128)S(1)}, f32[128,640]{1,0:T(8,128)S(1)}, u32[]{:S(2)}, u32[]{:S(2)}) %collective-permute-start) | collective-permute-done | bytes 327712 | tf_op jit(solution)/shard_map/ppermute | solution.py:292
  102.4 20.8 %all_to_all.48 = f32[128,1,640]{2,1,0:T(1,128)S(1)} all-to-all(f32[128,1,640]{2,1,0:T(1,128)S(1)} %all_to_all.38), channel_id=1, replica_groups=mesh['x'=4,'z'=8,'y'=4,'core'=2] {'x','z','y'}, dimensions={0} | all-to-all | bytes 655360 | tf_op jit(solution)/shard_map/all_to_all | solution.py:293
  (52 shorter events, 10.6 us)
Async XLA Ops:
  6.2 15.0 %all-to-all-start.2 = ((f32[16,1,4096]{2,1,0:T(1,128)}), f32[16,1,4096]{2,1,0:T(1,128)S(1)}, u32[]{:S(2)}, u32[]{:S(2)}) async-start(f32[16,1,4096]{2,1,0:T(1,128)} %bitcast.17), calls=%async_computation.2 | async-start | bytes 524288 | tf_op jit(solution)/shard_map/all_to_all | solution.py:243
  22.4 17.7 %all-to-all-start.3 = ((f32[8,2,4096]{2,1,0:T(2,128)}), f32[8,2,4096]{2,1,0:T(2,128)S(1)}, u32[]{:S(2)}, u32[]{:S(2)}) async-start(f32[8,2,4096]{2,1,0:T(2,128)} %broadcast_in_dim.141), calls=%async_computation.3 | async-start | bytes 524288 | tf_op jit(solution)/shard_map/all_to_all | solution.py:253
  42.0 9.6 %copy-start.7 = (s32[64,128]{1,0:T(8,128)S(1)}, s32[64,128]{1,0:T(8,128)}, u32[]{:S(2)}) copy-start(s32[64,128]{1,0:T(8,128)} %param.13) | copy-start | bytes 98308
  42.0 10.1 %copy-start.8 = (s32[1024]{0:T(1024)S(1)}, s32[1024]{0:T(1024)}, u32[]{:S(2)}) copy-start(s32[1024]{0:T(1024)} %param.14) | copy-start | bytes 12292
  42.0 11.7 %copy-start.3 = (f32[2,128,128]{2,1,0:T(8,128)S(1)}, f32[2,128,128]{2,1,0:T(8,128)}, u32[]{:S(2)}) copy-start(f32[2,128,128]{2,1,0:T(8,128)} %constant.231.clone.gain_ref) | copy-start | bytes 393220
  42.1 31.2 %all-to-all-start.4 = ((f32[16,8,4096]{2,1,0:T(8,128)}), f32[16,8,4096]{2,1,0:T(8,128)S(1)}, u32[]{:S(2)}, u32[]{:S(2)}) async-start(f32[16,8,4096]{2,1,0:T(8,128)} %broadcast_in_dim.142), calls=%async_computation.4 | async-start | bytes 4194304 | tf_op jit(solution)/shard_map/all_to_all | solution.py:260
  53.8 2.2 %copy-start = (bf16[16,512,256]{2,1,0:T(8,128)(2,1)S(1)}, bf16[16,512,256]{2,1,0:T(8,128)(2,1)}, u32[]{:S(2)}) copy-start(bf16[16,512,256]{2,1,0:T(8,128)(2,1)} %constant.227.clone.th_ref) | copy-start | bytes 12582916
  56.0 2.2 %copy-start.2 = (bf16[16,512,256]{2,1,0:T(8,128)(2,1)S(1)}, bf16[16,512,256]{2,1,0:T(8,128)(2,1)}, u32[]{:S(2)}) copy-start(bf16[16,512,256]{2,1,0:T(8,128)(2,1)} %constant.228.clone.tl_ref) | copy-start | bytes 12582916
  68.1 1.9 %copy-start.6 = (bf16[128,128,128]{2,1,0:T(8,128)(2,1)}, bf16[128,128,128]{2,1,0:T(8,128)(2,1)S(1)}, u32[]{:S(2)}) copy-start(bf16[128,128,128]{2,1,0:T(8,128)(2,1)S(1)} %shard_map.91.a_ref) | copy-start | bytes 12582916
  70.0 4.8 %copy-start.4 = (bf16[256,128]{1,0:T(8,128)(2,1)S(1)}, bf16[256,128]{1,0:T(8,128)(2,1)}, u32[]{:S(2)}) copy-start(bf16[256,128]{1,0:T(8,128)(2,1)} %constant.229.clone.bh_ref) | copy-start | bytes 196612
  70.0 4.8 %copy-start.5 = (bf16[256,128]{1,0:T(8,128)(2,1)S(1)}, bf16[256,128]{1,0:T(8,128)(2,1)}, u32[]{:S(2)}) copy-start(bf16[256,128]{1,0:T(8,128)(2,1)} %constant.230.clone.bl_ref) | copy-start | bytes 196612
  74.8 2.2 %copy-start.1 = (bf16[16,512,256]{2,1,0:T(8,128)(2,1)S(1)}, bf16[16,512,256]{2,1,0:T(8,128)(2,1)}, u32[]{:S(2)}) copy-start(bf16[16,512,256]{2,1,0:T(8,128)(2,1)} %constant.227.clone.th_ref) | copy-start | bytes 12582916
  95.2 6.9 %collective-permute-start = (f32[128,640]{1,0:T(8,128)S(1)}, f32[128,640]{1,0:T(8,128)S(1)}, u32[]{:S(2)}, u32[]{:S(2)}) collective-permute-start(f32[128,640]{1,0:T(8,128)S(1)} %bitcast.76), channel_id=1, source_target_pairs={{0,1},{1,0},{2,3},{3,2},{4,5},{5,4},{6,7},{7,6},{8,9},{9,8},{10,11... | collective-permute-start | bytes 983048 | tf_op jit(solution)/shard_map/ppermute | solution.py:292
where the time goes:
time: 125 us; the launch traced here: 124 us
  starting transfers between devices  27.4 us (22%)
  Pallas kernels  26.9 us (22%)
  blocking collectives  20.8 us (17%)
  local copies, waits for them, and re-layouts  17.9 us (14%)
  waiting for transfers between devices  13.2 us (11%)
  other arithmetic  12.1 us (10%)
  between operations  2.92 us (2%)
  matrix products  2.91 us (2%)
    all_to_all x1, blocking collectives, per_device(): total = jnp.sum(lax.all_to_all(halves, CHIPS, 0, 0, tiled=True), axis=0)  20.8 us
    pallas_call x1, Pallas kernels, stacked(): pl.pallas_call(stack_kernel, out_shape=jax.ShapeDtypeStruct((slots, LAGS)...  16.9 us
    unnamed x20, local copies, waits for them, and re-layouts  10.3 us
    pallas_call x1, Pallas kernels, receiver_side(): pl.pallas_call(receiver_kernel, out_shape=jax.ShapeDtypeStruct((HALF, 2 *...  9.92 us
    all_to_all x1, starting transfers between devices, per_device(): lax.all_to_all(wide, 'z', 0, 0, tiled=True).reshape(Z * ROUNDS, 2 * bins)  8.18 us
    all_to_all x1, starting transfers between devices, per_device(): came = lax.all_to_all(picked, PLANE, 0, 0, tiled=True)  7.58 us
    all_to_all x1, waiting for transfers between devices, per_device(): lax.all_to_all(wide, 'z', 0, 0, tiled=True).reshape(Z * ROUNDS, 2 * bins)  7.11 us
    all_to_all x1, starting transfers between devices, per_device(): lax.all_to_all(wide, PLANE, 0, 0, tiled=True).reshape(count, 2 * bins)  5.94 us
  transfers between devices with their start and end apart: 4, of which 4 were waited for; matrix products, arithmetic and copies ran while one was open for 9% of the time, Pallas kernels for 8%

commit v1 on v0

--- a/solution.py
+++ b/solution.py
@@ -21,6 +21,7 @@
 PLANE = ("x", "y")
 CHIPS = ("x", "z", "y")
 ROUNDS = 2
+GROUPS = 2
 highest = lax.Precision.HIGHEST
 
 
@@ -81,14 +82,32 @@
     return high, (values - high.astype(jnp.float32)).astype(jnp.bfloat16)
 
 
-def stack_kernel(z_ref, th_ref, tl_ref, a_ref, bins_ref, slot_ref, bh_ref, bl_ref, out_ref, w_ref, p_ref, acc_ref):
+def stack_kernel(
+    sources, high, low, receivers, bins_ref, slot_ref, bh_ref, bl_ref,
+    out_ref, w_ref, p_ref, acc_ref, z_ref, th_ref, tl_ref, a_ref, sems,
+):
     local = bins_ref.shape[0]
+    group = CLASSES // GROUPS
+    whole = [(sources, z_ref)]
+    for g in range(GROUPS):
+        part = pl.ds(g * group, group)
+        whole += [(high.at[part], th_ref.at[part]), (low.at[part], tl_ref.at[part])]
+    whole += [(receivers, a_ref)]
+    copies = [pltpu.make_async_copy(a, b, sems.at[i]) for i, (a, b) in enumerate(whole)]
+    for copy in copies:
+        copy.start()
+    copies[0].wait()
 
     for p in range(CLASSES):
+        if p % group == 0:
+            copies[1 + 2 * (p // group)].wait()
+            copies[2 + 2 * (p // group)].wait()
         zh, zl = split_here(z_ref[:, p * 2 * WIDTH : (p + 1) * 2 * WIDTH])
         u = nt(th_ref[p], zh) + nt(tl_ref[p], zh) + nt(th_ref[p], zl)
         for c in range(4):
             w_ref[pl.ds(c * CLASSES + p, HALF, stride=W_STEP), :] = u[c * HALF : (c + 1) * HALF]
+
+    copies[-1].wait()
 
     @pl.loop(0, HALF, unroll=16)
     def _(f):
@@ -98,13 +117,13 @@
         p_ref[pl.ds(f + HALF, local, stride=P_STEP), :] = o[local:]
 
     acc_ref[...] = jnp.zeros_like(acc_ref)
-    group = 8
-
-    @pl.loop(0, local // group)
+    some = 8
+
+    @pl.loop(0, local // some)
     def _(g):
         member, prod = [], []
-        for i in range(group):
-            r = g * group + i
+        for i in range(some):
+            r = g * some + i
             mine = slot_ref[...] == bins_ref[pl.ds(r, 1), :]
             member.append(jnp.where(mine, 1.0, 0.0).astype(jnp.bfloat16))
             prod.append(p_ref[pl.ds(pl.multiple_of(r * P_STEP, 8), FFT), :].astype(jnp.bfloat16))
@@ -125,14 +144,19 @@
     return pl.pallas_call(
         stack_kernel,
         out_shape=jax.ShapeDtypeStruct((slots, LAGS), jnp.float32),
-        in_specs=[vmem] * 8,
+        in_specs=[pl.BlockSpec(memory_space=pl.ANY)] * 4 + [vmem] * 4,
         out_specs=vmem,
         scratch_shapes=[
             pltpu.VMEM((HALF * W_STEP, 128), jnp.float32),
             pltpu.VMEM((local * P_STEP, 128), jnp.float32),
             pltpu.VMEM((slots, FFT), jnp.float32),
+            pltpu.VMEM(sources.shape, jnp.float32),
+            pltpu.VMEM(spread_h.shape, jnp.bfloat16),
+            pltpu.VMEM(spread_h.shape, jnp.bfloat16),
+            pltpu.VMEM(receivers.shape, jnp.bfloat16),
+            pltpu.SemaphoreType.DMA((2 * GROUPS + 2,)),
         ],
-        compiler_params=pltpu.CompilerParams(vmem_limit_bytes=48 * 1024 * 1024),
+        compiler_params=pltpu.CompilerParams(vmem_limit_bytes=50 * 1024 * 1024),
         cost_estimate=pl.CostEstimate(flops=9 * 10**9, bytes_accessed=16 * 2**20, transcendentals=0),
     )(sources, spread_h, spread_l, receivers, bins, bin_of, back_h, back_l)
 
@@ -184,7 +208,7 @@
         in_specs=[vmem] * 4,
         out_specs=vmem,
         scratch_shapes=[pltpu.VMEM((width, 128), jnp.float32), pltpu.VMEM((HALF * W_STEP, 128), jnp.float32)],
-        compiler_params=pltpu.CompilerParams(vmem_limit_bytes=40 * 1024 * 1024),
+        compiler_params=pltpu.CompilerParams(vmem_limit_bytes=26 * 1024 * 1024),
         cost_estimate=pl.CostEstimate(flops=6 * 10**9, bytes_accessed=14 * 2**20, transcendentals=0),
     )(flat, spread_h, spread_l, gain)
 
@@ -244,7 +268,8 @@
 
     before = jnp.sum((plane[None, :] < lax.broadcasted_iota(jnp.int32, (Z, 1), 0)).astype(jnp.int32), axis=1)
     first = before + (my_spot - before) % spots
-    turn = (rank - first[plane]) // spots
+    first_of = jnp.sum(jnp.where(plane[:, None] == lax.broadcasted_iota(jnp.int32, (1, Z), 1), first[None, :], 0), axis=1)
+    turn = (rank - first_of) // spots
     here = (plane == my_plane) & (dest == my_spot)
     at = here[None, :] & (turn[None, :] == lax.broadcasted_iota(jnp.int32, (ROUNDS, 1), 0))
     sender = jnp.max(jnp.where(at, spot[None, :], -1), axis=1)
@@ -255,30 +280,32 @@
     at = rank[None, :] == lax.broadcasted_iota(jnp.int32, (rows, 1), 0) * spots + my_spot
     sender = jnp.max(jnp.where(at, (plane * ROUNDS + turn)[None, :], -1), axis=1)
     kept = select_rows(sender[:, None] == lax.broadcasted_iota(jnp.int32, (1, Z * ROUNDS), 1), came)
-    kept, later = lax.optimization_barrier((kept, flat))
-    wide = jnp.broadcast_to(kept[None], (spots,) + kept.shape)
-    routed = lax.all_to_all(wide, PLANE, 0, 0, tiled=True).reshape(count, 2 * bins)
-    receivers = receiver_side(later, spread_h, spread_l, jnp.asarray(gain, jnp.float32))
-
-    place = dest * rows + rank // spots
-    placing = place[:, None] == lax.broadcasted_iota(jnp.int32, (count, count), 1)
-
-    def summed():
-        ids = jnp.sum(jnp.where(placing, mine[:, None], 0), axis=0)
+
+    def dense():
+        t = lax.iota(jnp.int32, count)
+        _, z, d = where_of(t, 1)
+        ids = jnp.sum(jnp.where(rank[None, :] == (z * spots + d)[:, None], mine[None, :], 0), axis=1)
         chan_ids = ch_rank * local + lax.broadcasted_iota(jnp.int32, (1, local), 1)
         found = select_rows(ids[:, None] == chan_ids, flat)
         home = jnp.sum(lax.all_to_all(found, CHIPS, 0, 0, tiled=True), axis=0, keepdims=True)
         home = by_class(home.reshape(1, 2, bins)).reshape(1, 2 * bins)
-        return lax.all_to_all(jnp.broadcast_to(home, (count, 2 * bins)), CHIPS, 0, 0, tiled=True)
+        return lax.all_to_all(jnp.broadcast_to(home, (rows, 2 * bins)), "z", 0, 0, tiled=True)
 
     ok = fits(source_ids[:count], local) & fits(source_ids[count:], local)
-    sources = lax.cond(ok, lambda: routed, summed)
-
+    kept = lax.cond(ok, lambda: kept, dense)
+    place = dest * rows + rank // spots
+    placing = place[:, None] == lax.broadcasted_iota(jnp.int32, (count, count), 1)
     iota = lax.broadcasted_iota(jnp.int32, (slots, 1), 0)
     bin_of = jnp.sum(jnp.where(iota == owner_slots[None, :], lax.broadcasted_iota(jnp.int32, (1, slots), 1), 0), axis=1)
     bins_here = select_rows(offset_bins, placing.astype(jnp.float32)).astype(jnp.int32)
     counts = bin_counts(offset_bins, slots, owner_slots)
     bin_wide = jnp.broadcast_to(bin_of[:, None], (slots, 128))
+    kept, later, bins_here, counts, bin_wide = lax.optimization_barrier((kept, flat, bins_here, counts, bin_wide))
+    wide = jnp.broadcast_to(kept[None], (spots,) + kept.shape)
+    sources = lax.all_to_all(wide, PLANE, 0, 0, tiled=True).reshape(count, 2 * bins)
+    receivers = receiver_side(later, spread_h, spread_l, jnp.asarray(gain, jnp.float32))
+
+
     panel = stacked(sources, spread_h, spread_l, receivers, bins_here, bin_wide, back_h, back_l)
 
     devices = X * Y * Z

time: 125 us -> 118 us (0.944)
  other arithmetic: 12.1 us -> 6.99 us
  waiting for transfers between devices: 13.2 us -> 17.2 us
  local copies, waits for them, and re-layouts: 17.9 us -> 14.4 us
  starting transfers between devices: 27.4 us -> 25.6 us
    add x1, other arithmetic: 5 us -> 0.02 us  [per_device(): plane * ROUNDS + turn]
    all_to_all x1, waiting for transfers between devices: 1.51 us -> 5.97 us  [per_device(): came = lax.all_to_all(picked, PLANE, 0, 0, tiled=True)]
    all_to_all x1, waiting for transfers between devices: 7.11 us -> 3.32 us  [per_device(): lax.all_to_all(wide, 'z', 0, 0, tiled=True).reshape(Z * ROUNDS, 2 * bins)]
    all_to_all x1, waiting for transfers between devices: 3.29 us -> 6.67 us  [per_device(): lax.all_to_all(wide, PLANE, 0, 0, tiled=True).reshape(count, 2 * bins)]
    all_to_all x1, starting transfers between devices: 5.94 us -> 3.72 us  [per_device(): lax.all_to_all(wide, PLANE, 0, 0, tiled=True).reshape(count, 2 * bins)]
    unnamed x20 -> x22, local copies, waits for them, and re-layouts: 10.3 us -> 8.2 us
    pallas_call x1, Pallas kernels: 16.9 us -> 15.5 us  [stacked(): pl.pallas_call(stack_kernel, out_shape=jax.ShapeDtypeStruct((slots, LAGS)...]
    cond x1 -> x0, local copies, waits for them, and re-layouts: 1.33 us -> none
  transfers between devices with their start and end apart: 4 -> 4, of which waited for: 4 -> 4; matrix products, arithmetic and copies ran while one was open for 9% -> 5% of each run, Pallas kernels for 8% -> 9%
where the time goes in v1:
time: 118 us
  Pallas kernels  26.6 us (23%)
  starting transfers between devices  25.6 us (22%)
  blocking collectives  21 us (18%)
  waiting for transfers between devices  17.2 us (15%)
  local copies, waits for them, and re-layouts  14.4 us (12%)
  other arithmetic  6.99 us (6%)
  matrix products  2.91 us (2%)
  between operations  2.81 us (2%)
    all_to_all x1, blocking collectives, per_device(): total = jnp.sum(lax.all_to_all(halves, CHIPS, 0, 0, tiled=True), axis=0)  21 us
    pallas_call x1, Pallas kernels, stacked(): pl.pallas_call(stack_kernel, out_shape=jax.ShapeDtypeStruct((slots, LAGS)...  15.5 us
    pallas_call x1, Pallas kernels, receiver_side(): pl.pallas_call(receiver_kernel, out_shape=jax.ShapeDtypeStruct((HALF, 2 *...  11.2 us
    unnamed x22, local copies, waits for them, and re-layouts  8.2 us
    all_to_all x1, starting transfers between devices, per_device(): lax.all_to_all(wide, 'z', 0, 0, tiled=True).reshape(Z * ROUNDS, 2 * bins)  8.19 us
    all_to_all x1, starting transfers between devices, per_device(): came = lax.all_to_all(picked, PLANE, 0, 0, tiled=True)  7.58 us
    all_to_all x1, waiting for transfers between devices, per_device(): lax.all_to_all(wide, PLANE, 0, 0, tiled=True).reshape(count, 2 * bins)  6.67 us
    ppermute x1, starting transfers between devices, per_device(): halves = here + lax.ppermute(there, 'core', [(0, 1), (1, 0)])  6.14 us
  transfers between devices with their start and end apart: 4, of which 4 were waited for; matrix products, arithmetic and copies ran while one was open for 5% of the time, Pallas kernels for 9%

profile of v1, /device:TPU:1, one launch (start us, length us, event | category | flops | bytes accessed | tf_op | source)
XLA Modules:
  0.0 117.8 jit_solution(16609625822926889750)
XLA Ops:
  0.0 0.9 compare_select_fusion.11
  1.1 1.8 %copy.32 = f32[8,8,2,2048]{3,1,2,0:T(8,128)S(1)} copy(f32[8,8,2,2048]{3,2,1,0:T(2,128)} %bitcast.66) | data formatting | bytes 2097152
  3.9 1.7 %fusion.10 = f32[16,16,2,128]{3,0,1,2:T(8,128)S(1)} fusion(f32[2,128,16,64]{3,2,1,0:T(8,128)S(1)} %bitcast.65, s32[16]{0:T(128)S(1)} %select_reduce_fusion.3), kind=kOutput, calls=%fused_computation.29 | convolution fusion | flops 50332672 | bytes 1310784 | tf_op jit(solution)/shard_map/dot_general | solution.py:229
  5.6 0.9 copy.25
  6.5 7.6 %all-to-all-start.2 = ((f32[16,1,4096]{2,1,0:T(1,128)}), f32[16,1,4096]{2,1,0:T(1,128)S(1)}, u32[]{:S(2)}, u32[]{:S(2)}) async-start(f32[16,1,4096]{2,1,0:T(1,128)} %bitcast.8), calls=%async_computation.2 | async-start | bytes 524288 | tf_op jit(solution)/shard_map/all_to_all | solution.py:267
  15.6 6.0 %all-to-all-done.2 = f32[16,1,4096]{2,1,0:T(1,128)S(1)} async-done(((f32[16,1,4096]{2,1,0:T(1,128)}), f32[16,1,4096]{2,1,0:T(1,128)S(1)}, u32[]{:S(2)}, u32[]{:S(2)}) %all-to-all-start.2) | async-done | bytes 262176 | tf_op jit(solution)/shard_map/all_to_all | solution.py:267
  21.9 0.8 broadcast_in_dim.155
  22.7 8.2 %all-to-all-start.3 = ((f32[8,2,4096]{2,1,0:T(2,128)}), f32[8,2,4096]{2,1,0:T(2,128)S(1)}, u32[]{:S(2)}, u32[]{:S(2)}) async-start(f32[8,2,4096]{2,1,0:T(2,128)} %broadcast_in_dim.155), calls=%async_computation.3 | async-start | bytes 524288 | tf_op jit(solution)/shard_map/all_to_all | solution.py:278
  31.1 0.7 reduce_max.63
  34.9 0.7 reduce_max.66
  37.1 3.3 %all-to-all-done.3 = f32[8,2,4096]{2,1,0:T(2,128)S(1)} async-done(((f32[8,2,4096]{2,1,0:T(2,128)}), f32[8,2,4096]{2,1,0:T(2,128)S(1)}, u32[]{:S(2)}, u32[]{:S(2)}) %all-to-all-start.3) | async-done | bytes 262176 | tf_op jit(solution)/shard_map/all_to_all | solution.py:278
  41.2 1.5 %broadcast_in_dim.162 = f32[16,8,4096]{2,1,0:T(8,128)} broadcast(f32[8,4096]{1,0:T(8,128)S(1)} %get-tuple-element.59), dimensions={1,2} | broadcast | bytes 2228224 | tf_op jit(solution)/shard_map/broadcast_in_dim | solution.py:304
  42.8 3.7 %all-to-all-start.4 = ((f32[16,8,4096]{2,1,0:T(8,128)}), f32[16,8,4096]{2,1,0:T(8,128)S(1)}, u32[]{:S(2)}, u32[]{:S(2)}) async-start(f32[16,8,4096]{2,1,0:T(8,128)} %broadcast_in_dim.162), calls=%async_computation.4 | async-start | bytes 4194304 | tf_op jit(solution)/shard_map/all_to_all | solution.py:305
  46.5 0.9 reshape.300
  47.4 2.2 %copy-done = bf16[16,512,256]{2,1,0:T(8,128)(2,1)S(1)} copy-done((bf16[16,512,256]{2,1,0:T(8,128)(2,1)S(1)}, bf16[16,512,256]{2,1,0:T(8,128)(2,1)}, u32[]{:S(2)}) %copy-start) | copy-done | bytes 4194328
  49.6 2.2 %copy-done.1 = bf16[16,512,256]{2,1,0:T(8,128)(2,1)S(1)} copy-done((bf16[16,512,256]{2,1,0:T(8,128)(2,1)S(1)}, bf16[16,512,256]{2,1,0:T(8,128)(2,1)}, u32[]{:S(2)}) %copy-start.1) | copy-done | bytes 4194328
  51.8 11.2 %shard_map.91.receivers = bf16[128,128,128]{2,1,0:T(8,128)(2,1)S(1)} custom-call(f32[64,4096]{1,0:T(8,128)} %bitcast.64, bf16[16,512,256]{2,1,0:T(8,128)(2,1)S(1)} %copy-done, bf16[16,512,256]{2,1,0:T(8,128)(2,1)S(1)} %copy-done.1, f32[2,128,128]{2,1,0:T(8,128)S(1)} %copy-done.2), custom_call_target="tpu_custom_call" | custom-call | flops 6000000000 | bytes 14680064 | tf_op jit(solution)/shard_map/pallas_call | solution.py:205
  63.0 1.9 %copy-done.5 = bf16[128,128,128]{2,1,0:T(8,128)(2,1)} copy-done((bf16[128,128,128]{2,1,0:T(8,128)(2,1)}, bf16[128,128,128]{2,1,0:T(8,128)(2,1)S(1)}, u32[]{:S(2)}) %copy-start.5) | copy-done | bytes 4194328
  64.9 6.7 %all-to-all-done.4 = f32[16,8,4096]{2,1,0:T(8,128)S(1)} async-done(((f32[16,8,4096]{2,1,0:T(8,128)}), f32[16,8,4096]{2,1,0:T(8,128)S(1)}, u32[]{:S(2)}, u32[]{:S(2)}) %all-to-all-start.4) | async-done | bytes 2097184 | tf_op jit(solution)/shard_map/all_to_all | solution.py:305
  71.6 15.5 %shard_map.92 = f32[1024,128]{1,0:T(8,128)S(1)} custom-call(f32[128,4096]{1,0:T(8,128)S(1)} %bitcast.61, bf16[16,512,256]{2,1,0:T(8,128)(2,1)} %constant.284.clone.th_ref.high, bf16[16,512,256]{2,1,0:T(8,128)(2,1)} %constant.285.clone.tl_ref.low, bf16[128,128,128]{2,1,0:T(8,128)(2,1)} %copy-done.5, s32[64,128]{1,0:T(8,128)S(1)} %fusion.13.bins_ref, ...), custom_call_target="tpu_custom_call" | custom-call | flops 8999999488 | bytes 16777216 | tf_op jit(solution)/shard_map/pallas_call | solution.py:144
  88.2 6.1 %collective-permute-start = (f32[128,640]{1,0:T(8,128)S(1)}, f32[128,640]{1,0:T(8,128)S(1)}, u32[]{:S(2)}, u32[]{:S(2)}) collective-permute-start(f32[128,640]{1,0:T(8,128)S(1)} %bitcast.69), channel_id=1, source_target_pairs={{0,1},{1,0},{2,3},{3,2},{4,5},{5,4},{6,7},{7,6},{8,9},{9,8},{10,11... | collective-permute-start | bytes 983048 | tf_op jit(solution)/shard_map/ppermute | solution.py:319
  94.4 1.3 %collective-permute-done = f32[128,640]{1,0:T(8,128)S(1)} collective-permute-done((f32[128,640]{1,0:T(8,128)S(1)}, f32[128,640]{1,0:T(8,128)S(1)}, u32[]{:S(2)}, u32[]{:S(2)}) %collective-permute-start) | collective-permute-done | bytes 327712 | tf_op jit(solution)/shard_map/ppermute | solution.py:319
  95.9 21.0 %all_to_all.47 = f32[128,1,640]{2,1,0:T(1,128)S(1)} all-to-all(f32[128,1,640]{2,1,0:T(1,128)S(1)} %all_to_all.37), channel_id=1, replica_groups=mesh['x'=4,'z'=8,'y'=4,'core'=2] {'x','z','y'}, dimensions={0} | all-to-all | bytes 655360 | tf_op jit(solution)/shard_map/all_to_all | solution.py:320
  117.2 0.7 bitcast_divide_fusion
  (52 shorter events, 7.7 us)
Async XLA Ops:
  1.1 13.1 %copy-start.8 = (s32[64,128]{1,0:T(8,128)S(1)}, s32[64,128]{1,0:T(8,128)}, u32[]{:S(2)}) copy-start(s32[64,128]{1,0:T(8,128)} %param.13) | copy-start | bytes 98308
  1.1 13.1 %copy-start.9 = (s32[1024]{0:T(1024)S(1)}, s32[1024]{0:T(1024)}, u32[]{:S(2)}) copy-start(s32[1024]{0:T(1024)} %param.14) | copy-start | bytes 12292
  2.9 37.9 %copy-start.6 = (f32[8,8,2,2048]{3,1,2,0:T(8,128)}, f32[8,8,2,2048]{3,1,2,0:T(8,128)S(1)}, u32[]{:S(2)}) copy-start(f32[8,8,2,2048]{3,1,2,0:T(8,128)S(1)} %copy.32) | copy-start | bytes 3145732
  6.5 15.0 %all-to-all-start.2 = ((f32[16,1,4096]{2,1,0:T(1,128)}), f32[16,1,4096]{2,1,0:T(1,128)S(1)}, u32[]{:S(2)}, u32[]{:S(2)}) async-start(f32[16,1,4096]{2,1,0:T(1,128)} %bitcast.8), calls=%async_computation.2 | async-start | bytes 524288 | tf_op jit(solution)/shard_map/all_to_all | solution.py:267
  22.7 17.7 %all-to-all-start.3 = ((f32[8,2,4096]{2,1,0:T(2,128)}), f32[8,2,4096]{2,1,0:T(2,128)S(1)}, u32[]{:S(2)}, u32[]{:S(2)}) async-start(f32[8,2,4096]{2,1,0:T(2,128)} %broadcast_in_dim.155), calls=%async_computation.3 | async-start | bytes 524288 | tf_op jit(solution)/shard_map/all_to_all | solution.py:278
  41.0 6.4 %copy-start.2 = (f32[2,128,128]{2,1,0:T(8,128)S(1)}, f32[2,128,128]{2,1,0:T(8,128)}, u32[]{:S(2)}) copy-start(f32[2,128,128]{2,1,0:T(8,128)} %constant.288.clone.gain_ref) | copy-start | bytes 393220
  42.8 28.8 %all-to-all-start.4 = ((f32[16,8,4096]{2,1,0:T(8,128)}), f32[16,8,4096]{2,1,0:T(8,128)S(1)}, u32[]{:S(2)}, u32[]{:S(2)}) async-start(f32[16,8,4096]{2,1,0:T(8,128)} %broadcast_in_dim.162), calls=%async_computation.4 | async-start | bytes 4194304 | tf_op jit(solution)/shard_map/all_to_all | solution.py:305
  47.4 2.2 %copy-start = (bf16[16,512,256]{2,1,0:T(8,128)(2,1)S(1)}, bf16[16,512,256]{2,1,0:T(8,128)(2,1)}, u32[]{:S(2)}) copy-start(bf16[16,512,256]{2,1,0:T(8,128)(2,1)} %constant.284.clone.th_ref.high) | copy-start | bytes 12582916
  49.6 2.2 %copy-start.1 = (bf16[16,512,256]{2,1,0:T(8,128)(2,1)S(1)}, bf16[16,512,256]{2,1,0:T(8,128)(2,1)}, u32[]{:S(2)}) copy-start(bf16[16,512,256]{2,1,0:T(8,128)(2,1)} %constant.285.clone.tl_ref.low) | copy-start | bytes 12582916
  51.8 19.8 %copy-start.3 = (bf16[256,128]{1,0:T(8,128)(2,1)S(1)}, bf16[256,128]{1,0:T(8,128)(2,1)}, u32[]{:S(2)}) copy-start(bf16[256,128]{1,0:T(8,128)(2,1)} %constant.286.clone.bh_ref) | copy-start | bytes 196612
  51.8 19.8 %copy-start.4 = (bf16[256,128]{1,0:T(8,128)(2,1)S(1)}, bf16[256,128]{1,0:T(8,128)(2,1)}, u32[]{:S(2)}) copy-start(bf16[256,128]{1,0:T(8,128)(2,1)} %constant.287.clone.bl_ref) | copy-start | bytes 196612
  63.0 1.9 %copy-start.5 = (bf16[128,128,128]{2,1,0:T(8,128)(2,1)}, bf16[128,128,128]{2,1,0:T(8,128)(2,1)S(1)}, u32[]{:S(2)}) copy-start(bf16[128,128,128]{2,1,0:T(8,128)(2,1)S(1)} %shard_map.91.receivers) | copy-start | bytes 12582916
  71.6 15.8 %copy-start.7 = (f32[128,2,4]{2,1,0:T(2,128)S(1)}, f32[128,2,4]{2,1,0:T(2,128)}, u32[]{:S(2)}) copy-start(f32[128,2,4]{2,1,0:T(2,128)} %reshape.300) | copy-start | bytes 12292
  88.2 7.4 %collective-permute-start = (f32[128,640]{1,0:T(8,128)S(1)}, f32[128,640]{1,0:T(8,128)S(1)}, u32[]{:S(2)}, u32[]{:S(2)}) collective-permute-start(f32[128,640]{1,0:T(8,128)S(1)} %bitcast.69), channel_id=1, source_target_pairs={{0,1},{1,0},{2,3},{3,2},{4,5},{5,4},{6,7},{7,6},{8,9},{9,8},{10,11... | collective-permute-start | bytes 983048 | tf_op jit(solution)/shard_map/ppermute | solution.py:319

commit v2 on v1

--- a/solution.py
+++ b/solution.py
@@ -21,7 +21,7 @@
 PLANE = ("x", "y")
 CHIPS = ("x", "z", "y")
 ROUNDS = 2
-GROUPS = 2
+GROUPS = 4
 highest = lax.Precision.HIGHEST
 
 
@@ -109,7 +109,7 @@
 
     copies[-1].wait()
 
-    @pl.loop(0, HALF, unroll=16)
+    @pl.loop(0, HALF, unroll=32)
     def _(f):
         w = w_ref[pl.ds(pl.multiple_of(f * W_STEP, 8), PARTS), :].astype(jnp.bfloat16)
         o = jnp.dot(a_ref[f], jnp.concatenate([w, w], axis=0), preferred_element_type=jnp.float32)
@@ -117,7 +117,7 @@
         p_ref[pl.ds(f + HALF, local, stride=P_STEP), :] = o[local:]
 
     acc_ref[...] = jnp.zeros_like(acc_ref)
-    some = 8
+    some = 16
 
     @pl.loop(0, local // some)
     def _(g):

time: 118 us -> 117 us (level)
  Pallas kernels: 26.6 us -> 24.9 us
    pallas_call x1, Pallas kernels: 15.5 us -> 13.7 us  [stacked(): pl.pallas_call(stack_kernel, out_shape=jax.ShapeDtypeStruct((slots, LAGS)...]
  transfers between devices with their start and end apart: 4 -> 4, of which waited for: 4 -> 4; matrix products, arithmetic and copies ran while one was open for 5% -> 5% of each run, Pallas kernels for 9% -> 10%
where the time goes in v2:
time: 117 us; the launch traced here: 116 us
  starting transfers between devices  25.6 us (22%)
  Pallas kernels  24.9 us (21%)
  blocking collectives  21 us (18%)
  waiting for transfers between devices  17.2 us (15%)
  local copies, waits for them, and re-layouts  14.4 us (12%)
  other arithmetic  6.99 us (6%)
  matrix products  2.91 us (2%)
  between operations  2.81 us (2%)
    all_to_all x1, blocking collectives, per_device(): total = jnp.sum(lax.all_to_all(halves, CHIPS, 0, 0, tiled=True), axis=0)  21 us
    pallas_call x1, Pallas kernels, stacked(): pl.pallas_call(stack_kernel, out_shape=jax.ShapeDtypeStruct((slots, LAGS)...  13.7 us
    pallas_call x1, Pallas kernels, receiver_side(): pl.pallas_call(receiver_kernel, out_shape=jax.ShapeDtypeStruct((HALF, 2 *...  11.2 us
    unnamed x22, local copies, waits for them, and re-layouts  8.2 us
    all_to_all x1, starting transfers between devices, per_device(): lax.all_to_all(wide, 'z', 0, 0, tiled=True).reshape(Z * ROUNDS, 2 * bins)  8.19 us
    all_to_all x1, starting transfers between devices, per_device(): came = lax.all_to_all(picked, PLANE, 0, 0, tiled=True)  7.58 us
    all_to_all x1, waiting for transfers between devices, per_device(): lax.all_to_all(wide, PLANE, 0, 0, tiled=True).reshape(count, 2 * bins)  6.67 us
    ppermute x1, starting transfers between devices, per_device(): halves = here + lax.ppermute(there, 'core', [(0, 1), (1, 0)])  6.14 us
  transfers between devices with their start and end apart: 4, of which 4 were waited for; matrix products, arithmetic and copies ran while one was open for 5% of the time, Pallas kernels for 10%

profile of v2, /device:TPU:1, one launch (start us, length us, event | category | flops | bytes accessed | tf_op | source)
XLA Modules:
  0.0 116.1 jit_solution(10603347808072231788)
XLA Ops:
  0.0 0.9 compare_select_fusion.11
  1.1 1.8 %copy.32 = f32[8,8,2,2048]{3,1,2,0:T(8,128)S(1)} copy(f32[8,8,2,2048]{3,2,1,0:T(2,128)} %bitcast.66) | data formatting | bytes 2097152
  3.9 1.7 %fusion.10 = f32[16,16,2,128]{3,0,1,2:T(8,128)S(1)} fusion(f32[2,128,16,64]{3,2,1,0:T(8,128)S(1)} %bitcast.65, s32[16]{0:T(128)S(1)} %select_reduce_fusion.3), kind=kOutput, calls=%fused_computation.29 | convolution fusion | flops 50332672 | bytes 1310784 | tf_op jit(solution)/shard_map/dot_general | solution.py:229
  5.6 0.9 copy.25
  6.5 7.6 %all-to-all-start.2 = ((f32[16,1,4096]{2,1,0:T(1,128)}), f32[16,1,4096]{2,1,0:T(1,128)S(1)}, u32[]{:S(2)}, u32[]{:S(2)}) async-start(f32[16,1,4096]{2,1,0:T(1,128)} %bitcast.8), calls=%async_computation.2 | async-start | bytes 524288 | tf_op jit(solution)/shard_map/all_to_all | solution.py:267
  15.6 6.0 %all-to-all-done.2 = f32[16,1,4096]{2,1,0:T(1,128)S(1)} async-done(((f32[16,1,4096]{2,1,0:T(1,128)}), f32[16,1,4096]{2,1,0:T(1,128)S(1)}, u32[]{:S(2)}, u32[]{:S(2)}) %all-to-all-start.2) | async-done | bytes 262176 | tf_op jit(solution)/shard_map/all_to_all | solution.py:267
  21.9 0.8 broadcast_in_dim.155
  22.7 8.2 %all-to-all-start.3 = ((f32[8,2,4096]{2,1,0:T(2,128)}), f32[8,2,4096]{2,1,0:T(2,128)S(1)}, u32[]{:S(2)}, u32[]{:S(2)}) async-start(f32[8,2,4096]{2,1,0:T(2,128)} %broadcast_in_dim.155), calls=%async_computation.3 | async-start | bytes 524288 | tf_op jit(solution)/shard_map/all_to_all | solution.py:278
  31.1 0.7 reduce_max.63
  34.9 0.7 reduce_max.66
  37.1 3.3 %all-to-all-done.3 = f32[8,2,4096]{2,1,0:T(2,128)S(1)} async-done(((f32[8,2,4096]{2,1,0:T(2,128)}), f32[8,2,4096]{2,1,0:T(2,128)S(1)}, u32[]{:S(2)}, u32[]{:S(2)}) %all-to-all-start.3) | async-done | bytes 262176 | tf_op jit(solution)/shard_map/all_to_all | solution.py:278
  41.2 1.5 %broadcast_in_dim.162 = f32[16,8,4096]{2,1,0:T(8,128)} broadcast(f32[8,4096]{1,0:T(8,128)S(1)} %get-tuple-element.59), dimensions={1,2} | broadcast | bytes 2228224 | tf_op jit(solution)/shard_map/broadcast_in_dim | solution.py:304
  42.8 3.7 %all-to-all-start.4 = ((f32[16,8,4096]{2,1,0:T(8,128)}), f32[16,8,4096]{2,1,0:T(8,128)S(1)}, u32[]{:S(2)}, u32[]{:S(2)}) async-start(f32[16,8,4096]{2,1,0:T(8,128)} %broadcast_in_dim.162), calls=%async_computation.4 | async-start | bytes 4194304 | tf_op jit(solution)/shard_map/all_to_all | solution.py:305
  46.5 0.9 reshape.300
  47.4 2.2 %copy-done = bf16[16,512,256]{2,1,0:T(8,128)(2,1)S(1)} copy-done((bf16[16,512,256]{2,1,0:T(8,128)(2,1)S(1)}, bf16[16,512,256]{2,1,0:T(8,128)(2,1)}, u32[]{:S(2)}) %copy-start) | copy-done | bytes 4194328
  49.6 2.2 %copy-done.1 = bf16[16,512,256]{2,1,0:T(8,128)(2,1)S(1)} copy-done((bf16[16,512,256]{2,1,0:T(8,128)(2,1)S(1)}, bf16[16,512,256]{2,1,0:T(8,128)(2,1)}, u32[]{:S(2)}) %copy-start.1) | copy-done | bytes 4194328
  51.8 11.2 %shard_map.91.receivers = bf16[128,128,128]{2,1,0:T(8,128)(2,1)S(1)} custom-call(f32[64,4096]{1,0:T(8,128)} %bitcast.64, bf16[16,512,256]{2,1,0:T(8,128)(2,1)S(1)} %copy-done, bf16[16,512,256]{2,1,0:T(8,128)(2,1)S(1)} %copy-done.1, f32[2,128,128]{2,1,0:T(8,128)S(1)} %copy-done.2), custom_call_target="tpu_custom_call" | custom-call | flops 6000000000 | bytes 14680064 | tf_op jit(solution)/shard_map/pallas_call | solution.py:205
  63.0 1.9 %copy-done.5 = bf16[128,128,128]{2,1,0:T(8,128)(2,1)} copy-done((bf16[128,128,128]{2,1,0:T(8,128)(2,1)}, bf16[128,128,128]{2,1,0:T(8,128)(2,1)S(1)}, u32[]{:S(2)}) %copy-start.5) | copy-done | bytes 4194328
  64.9 6.7 %all-to-all-done.4 = f32[16,8,4096]{2,1,0:T(8,128)S(1)} async-done(((f32[16,8,4096]{2,1,0:T(8,128)}), f32[16,8,4096]{2,1,0:T(8,128)S(1)}, u32[]{:S(2)}, u32[]{:S(2)}) %all-to-all-start.4) | async-done | bytes 2097184 | tf_op jit(solution)/shard_map/all_to_all | solution.py:305
  71.6 13.7 %shard_map.92 = f32[1024,128]{1,0:T(8,128)S(1)} custom-call(f32[128,4096]{1,0:T(8,128)S(1)} %bitcast.61, bf16[16,512,256]{2,1,0:T(8,128)(2,1)} %constant.284.clone.th_ref.high, bf16[16,512,256]{2,1,0:T(8,128)(2,1)} %constant.285.clone.tl_ref.low, bf16[128,128,128]{2,1,0:T(8,128)(2,1)} %copy-done.5, s32[64,128]{1,0:T(8,128)S(1)} %fusion.13.bins_ref, ...), custom_call_target="tpu_custom_call" | custom-call | flops 8999999488 | bytes 16777216 | tf_op jit(solution)/shard_map/pallas_call | solution.py:144
  86.5 6.1 %collective-permute-start = (f32[128,640]{1,0:T(8,128)S(1)}, f32[128,640]{1,0:T(8,128)S(1)}, u32[]{:S(2)}, u32[]{:S(2)}) collective-permute-start(f32[128,640]{1,0:T(8,128)S(1)} %bitcast.69), channel_id=1, source_target_pairs={{0,1},{1,0},{2,3},{3,2},{4,5},{5,4},{6,7},{7,6},{8,9},{9,8},{10,11... | collective-permute-start | bytes 983048 | tf_op jit(solution)/shard_map/ppermute | solution.py:319
  92.6 1.3 %collective-permute-done = f32[128,640]{1,0:T(8,128)S(1)} collective-permute-done((f32[128,640]{1,0:T(8,128)S(1)}, f32[128,640]{1,0:T(8,128)S(1)}, u32[]{:S(2)}, u32[]{:S(2)}) %collective-permute-start) | collective-permute-done | bytes 327712 | tf_op jit(solution)/shard_map/ppermute | solution.py:319
  94.2 21.0 %all_to_all.47 = f32[128,1,640]{2,1,0:T(1,128)S(1)} all-to-all(f32[128,1,640]{2,1,0:T(1,128)S(1)} %all_to_all.37), channel_id=1, replica_groups=mesh['x'=4,'z'=8,'y'=4,'core'=2] {'x','z','y'}, dimensions={0} | all-to-all | bytes 655360 | tf_op jit(solution)/shard_map/all_to_all | solution.py:320
  115.4 0.7 bitcast_divide_fusion
  (52 shorter events, 7.7 us)
Async XLA Ops:
  1.1 13.1 %copy-start.8 = (s32[64,128]{1,0:T(8,128)S(1)}, s32[64,128]{1,0:T(8,128)}, u32[]{:S(2)}) copy-start(s32[64,128]{1,0:T(8,128)} %param.13) | copy-start | bytes 98308
  1.1 13.1 %copy-start.9 = (s32[1024]{0:T(1024)S(1)}, s32[1024]{0:T(1024)}, u32[]{:S(2)}) copy-start(s32[1024]{0:T(1024)} %param.14) | copy-start | bytes 12292
  2.9 37.9 %copy-start.6 = (f32[8,8,2,2048]{3,1,2,0:T(8,128)}, f32[8,8,2,2048]{3,1,2,0:T(8,128)S(1)}, u32[]{:S(2)}) copy-start(f32[8,8,2,2048]{3,1,2,0:T(8,128)S(1)} %copy.32) | copy-start | bytes 3145732
  6.5 15.0 %all-to-all-start.2 = ((f32[16,1,4096]{2,1,0:T(1,128)}), f32[16,1,4096]{2,1,0:T(1,128)S(1)}, u32[]{:S(2)}, u32[]{:S(2)}) async-start(f32[16,1,4096]{2,1,0:T(1,128)} %bitcast.8), calls=%async_computation.2 | async-start | bytes 524288 | tf_op jit(solution)/shard_map/all_to_all | solution.py:267
  22.7 17.7 %all-to-all-start.3 = ((f32[8,2,4096]{2,1,0:T(2,128)}), f32[8,2,4096]{2,1,0:T(2,128)S(1)}, u32[]{:S(2)}, u32[]{:S(2)}) async-start(f32[8,2,4096]{2,1,0:T(2,128)} %broadcast_in_dim.155), calls=%async_computation.3 | async-start | bytes 524288 | tf_op jit(solution)/shard_map/all_to_all | solution.py:278
  41.0 6.4 %copy-start.2 = (f32[2,128,128]{2,1,0:T(8,128)S(1)}, f32[2,128,128]{2,1,0:T(8,128)}, u32[]{:S(2)}) copy-start(f32[2,128,128]{2,1,0:T(8,128)} %constant.288.clone.gain_ref) | copy-start | bytes 393220
  42.8 28.8 %all-to-all-start.4 = ((f32[16,8,4096]{2,1,0:T(8,128)}), f32[16,8,4096]{2,1,0:T(8,128)S(1)}, u32[]{:S(2)}, u32[]{:S(2)}) async-start(f32[16,8,4096]{2,1,0:T(8,128)} %broadcast_in_dim.162), calls=%async_computation.4 | async-start | bytes 4194304 | tf_op jit(solution)/shard_map/all_to_all | solution.py:305
  47.4 2.2 %copy-start = (bf16[16,512,256]{2,1,0:T(8,128)(2,1)S(1)}, bf16[16,512,256]{2,1,0:T(8,128)(2,1)}, u32[]{:S(2)}) copy-start(bf16[16,512,256]{2,1,0:T(8,128)(2,1)} %constant.284.clone.th_ref.high) | copy-start | bytes 12582916
  49.6 2.2 %copy-start.1 = (bf16[16,512,256]{2,1,0:T(8,128)(2,1)S(1)}, bf16[16,512,256]{2,1,0:T(8,128)(2,1)}, u32[]{:S(2)}) copy-start(bf16[16,512,256]{2,1,0:T(8,128)(2,1)} %constant.285.clone.tl_ref.low) | copy-start | bytes 12582916
  51.8 19.8 %copy-start.3 = (bf16[256,128]{1,0:T(8,128)(2,1)S(1)}, bf16[256,128]{1,0:T(8,128)(2,1)}, u32[]{:S(2)}) copy-start(bf16[256,128]{1,0:T(8,128)(2,1)} %constant.286.clone.bh_ref) | copy-start | bytes 196612
  51.8 19.8 %copy-start.4 = (bf16[256,128]{1,0:T(8,128)(2,1)S(1)}, bf16[256,128]{1,0:T(8,128)(2,1)}, u32[]{:S(2)}) copy-start(bf16[256,128]{1,0:T(8,128)(2,1)} %constant.287.clone.bl_ref) | copy-start | bytes 196612
  63.0 1.9 %copy-start.5 = (bf16[128,128,128]{2,1,0:T(8,128)(2,1)}, bf16[128,128,128]{2,1,0:T(8,128)(2,1)S(1)}, u32[]{:S(2)}) copy-start(bf16[128,128,128]{2,1,0:T(8,128)(2,1)S(1)} %shard_map.91.receivers) | copy-start | bytes 12582916
  71.6 14.0 %copy-start.7 = (f32[128,2,4]{2,1,0:T(2,128)S(1)}, f32[128,2,4]{2,1,0:T(2,128)}, u32[]{:S(2)}) copy-start(f32[128,2,4]{2,1,0:T(2,128)} %reshape.300) | copy-start | bytes 12292
  86.5 7.4 %collective-permute-start = (f32[128,640]{1,0:T(8,128)S(1)}, f32[128,640]{1,0:T(8,128)S(1)}, u32[]{:S(2)}, u32[]{:S(2)}) collective-permute-start(f32[128,640]{1,0:T(8,128)S(1)} %bitcast.69), channel_id=1, source_target_pairs={{0,1},{1,0},{2,3},{3,2},{4,5},{5,4},{6,7},{7,6},{8,9},{9,8},{10,11... | collective-permute-start | bytes 983048 | tf_op jit(solution)/shard_map/ppermute | solution.py:319

commit v3 on v2

--- a/solution.py
+++ b/solution.py
@@ -229,13 +229,13 @@
     return jnp.dot(table.astype(jnp.float32), rows, precision=highest, preferred_element_type=jnp.float32)
 
 
-def bin_counts(bins, slots, owner_slots):
+def bin_counts(bins, slots, owner_slots, slot_of):
     flat = bins.reshape(1, -1)
     digit = lax.broadcasted_iota(jnp.int32, (32, 1), 0)
     high = (flat // 32 == digit).astype(jnp.bfloat16)
     low = (flat % 32 == digit).astype(jnp.bfloat16)
     per_bin = nt(high, low).reshape(1, slots)
-    at = lax.broadcasted_iota(jnp.int32, (slots, 1), 0) == owner_slots[None, :]
+    at = slot_of == owner_slots[None, :]
     return jnp.sum(jnp.where(at, per_bin, 0.0), axis=1)
 
 
@@ -295,10 +295,14 @@
     kept = lax.cond(ok, lambda: kept, dense)
     place = dest * rows + rank // spots
     placing = place[:, None] == lax.broadcasted_iota(jnp.int32, (count, count), 1)
-    iota = lax.broadcasted_iota(jnp.int32, (slots, 1), 0)
-    bin_of = jnp.sum(jnp.where(iota == owner_slots[None, :], lax.broadcasted_iota(jnp.int32, (1, slots), 1), 0), axis=1)
+    devices = X * Y * Z
+    own = slots // (2 * devices)
+    line = lax.broadcasted_iota(jnp.int32, (slots, 1), 0)
+    block = devices * own
+    slot_of = (line % block // own * 2 + (line // block + src_rank) % 2) * own + line % own
+    bin_of = jnp.sum(jnp.where(slot_of == owner_slots[None, :], lax.broadcasted_iota(jnp.int32, (1, slots), 1), 0), axis=1)
     bins_here = select_rows(offset_bins, placing.astype(jnp.float32)).astype(jnp.int32)
-    counts = bin_counts(offset_bins, slots, owner_slots)
+    counts = bin_counts(offset_bins, slots, owner_slots, slot_of)
     bin_wide = jnp.broadcast_to(bin_of[:, None], (slots, 128))
     kept, later, bins_here, counts, bin_wide = lax.optimization_barrier((kept, flat, bins_here, counts, bin_wide))
     wide = jnp.broadcast_to(kept[None], (spots,) + kept.shape)
@@ -308,16 +312,13 @@
 
     panel = stacked(sources, spread_h, spread_l, receivers, bins_here, bin_wide, back_h, back_l)
 
-    devices = X * Y * Z
-    own = slots // (2 * devices)
-    packed = jnp.concatenate(
-        [panel.reshape(devices, 2, own * LAGS), jnp.pad(counts.reshape(devices, 2, own), ((0, 0), (0, 0), (0, LAGS - own)))],
-        axis=2,
+    counted = jnp.pad(counts.reshape(2, devices, own), ((0, 0), (0, 0), (0, LAGS - own)))
+    here, there = (
+        jnp.concatenate([panel[i * block : (i + 1) * block].reshape(devices, own * LAGS), counted[i]], axis=1)
+        for i in range(2)
     )
-    here = lax.dynamic_index_in_dim(packed, src_rank, 1, keepdims=False)
-    there = lax.dynamic_index_in_dim(packed, 1 - src_rank, 1, keepdims=False)
-    halves = here + lax.ppermute(there, "core", [(0, 1), (1, 0)])
-    total = jnp.sum(lax.all_to_all(halves, CHIPS, 0, 0, tiled=True), axis=0)
+    both = here + lax.ppermute(there, "core", [(0, 1), (1, 0)])
+    total = jnp.sum(lax.all_to_all(both, CHIPS, 0, 0, tiled=True), axis=0)
     stack_sum = total[: own * LAGS].reshape(own, LAGS)
     stack_count = total[own * LAGS : own * LAGS + own]
     return stack_sum / jnp.sqrt(jnp.maximum(stack_count, 1.0))[:, None]

time: 117 us -> 116 us (level)
  local copies, waits for them, and re-layouts: 14.4 us -> 12.9 us
    unnamed x22 -> x19, local copies, waits for them, and re-layouts: 8.2 us -> 8.16 us
where the time goes in v3:
time: 116 us; the launch traced here: 115 us
  starting transfers between devices  25.6 us (22%)
  Pallas kernels  24.9 us (21%)
  blocking collectives  21 us (18%)
  waiting for transfers between devices  17.6 us (15%)
  local copies, waits for them, and re-layouts  12.9 us (11%)
  other arithmetic  6.97 us (6%)
  matrix products  2.91 us (3%)
  between operations  2.82 us (2%)
    all_to_all x1, blocking collectives, per_device(): total = jnp.sum(lax.all_to_all(both, CHIPS, 0, 0, tiled=True), axis=0)  21 us
    pallas_call x1, Pallas kernels, stacked(): pl.pallas_call(stack_kernel, out_shape=jax.ShapeDtypeStruct((slots, LAGS)...  13.7 us
    pallas_call x1, Pallas kernels, receiver_side(): pl.pallas_call(receiver_kernel, out_shape=jax.ShapeDtypeStruct((HALF, 2 *...  11.2 us
    all_to_all x1, starting transfers between devices, per_device(): lax.all_to_all(wide, 'z', 0, 0, tiled=True).reshape(Z * ROUNDS, 2 * bins)  8.19 us
    unnamed x19, local copies, waits for them, and re-layouts  8.16 us
    all_to_all x1, starting transfers between devices, per_device(): came = lax.all_to_all(picked, PLANE, 0, 0, tiled=True)  7.58 us
    all_to_all x1, waiting for transfers between devices, per_device(): lax.all_to_all(wide, PLANE, 0, 0, tiled=True).reshape(count, 2 * bins)  7.38 us
    ppermute x1, starting transfers between devices, per_device(): both = here + lax.ppermute(there, 'core', [(0, 1), (1, 0)])  6.16 us
  transfers between devices with their start and end apart: 4, of which 4 were waited for; matrix products, arithmetic and copies ran while one was open for 5% of the time, Pallas kernels for 10%

profile of v3, /device:TPU:1, one launch (start us, length us, event | category | flops | bytes accessed | tf_op | source)
XLA Modules:
  0.0 115.0 jit_solution(2518927517660295187)
XLA Ops:
  0.0 0.9 compare_select_fusion.12
  1.3 1.8 %copy.30 = f32[8,8,2,2048]{3,1,2,0:T(8,128)S(1)} copy(f32[8,8,2,2048]{3,2,1,0:T(2,128)} %bitcast.65) | data formatting | bytes 2097152
  3.9 1.7 %fusion.12 = f32[16,16,2,128]{3,0,1,2:T(8,128)S(1)} fusion(f32[2,128,16,64]{3,2,1,0:T(8,128)S(1)} %bitcast.64, s32[16]{0:T(128)S(1)} %select_reduce_fusion.1), kind=kOutput, calls=%fused_computation.29 | convolution fusion | flops 50332672 | bytes 1310784 | tf_op jit(solution)/shard_map/dot_general | solution.py:229
  5.6 0.9 copy.25
  6.5 7.6 %all-to-all-start.2 = ((f32[16,1,4096]{2,1,0:T(1,128)}), f32[16,1,4096]{2,1,0:T(1,128)S(1)}, u32[]{:S(2)}, u32[]{:S(2)}) async-start(f32[16,1,4096]{2,1,0:T(1,128)} %bitcast.8), calls=%async_computation.2 | async-start | bytes 524288 | tf_op jit(solution)/shard_map/all_to_all | solution.py:267
  14.5 0.7 fusion.9
  15.8 5.8 %all-to-all-done.2 = f32[16,1,4096]{2,1,0:T(1,128)S(1)} async-done(((f32[16,1,4096]{2,1,0:T(1,128)}), f32[16,1,4096]{2,1,0:T(1,128)S(1)}, u32[]{:S(2)}, u32[]{:S(2)}) %all-to-all-start.2) | async-done | bytes 262176 | tf_op jit(solution)/shard_map/all_to_all | solution.py:267
  21.9 0.8 broadcast_in_dim.155
  22.7 8.2 %all-to-all-start.3 = ((f32[8,2,4096]{2,1,0:T(2,128)}), f32[8,2,4096]{2,1,0:T(2,128)S(1)}, u32[]{:S(2)}, u32[]{:S(2)}) async-start(f32[8,2,4096]{2,1,0:T(2,128)} %broadcast_in_dim.155), calls=%async_computation.3 | async-start | bytes 524288 | tf_op jit(solution)/shard_map/all_to_all | solution.py:278
  31.1 0.7 reduce_max.63
  34.9 0.7 reduce_max.66
  37.1 3.3 %all-to-all-done.3 = f32[8,2,4096]{2,1,0:T(2,128)S(1)} async-done(((f32[8,2,4096]{2,1,0:T(2,128)}), f32[8,2,4096]{2,1,0:T(2,128)S(1)}, u32[]{:S(2)}, u32[]{:S(2)}) %all-to-all-start.3) | async-done | bytes 262176 | tf_op jit(solution)/shard_map/all_to_all | solution.py:278
  41.2 1.5 %broadcast_in_dim.162 = f32[16,8,4096]{2,1,0:T(8,128)} broadcast(f32[8,4096]{1,0:T(8,128)S(1)} %get-tuple-element.61), dimensions={1,2} | broadcast | bytes 2228224 | tf_op jit(solution)/shard_map/broadcast_in_dim | solution.py:308
  42.8 3.7 %all-to-all-start.4 = ((f32[16,8,4096]{2,1,0:T(8,128)}), f32[16,8,4096]{2,1,0:T(8,128)S(1)}, u32[]{:S(2)}, u32[]{:S(2)}) async-start(f32[16,8,4096]{2,1,0:T(8,128)} %broadcast_in_dim.162), calls=%async_computation.4 | async-start | bytes 4194304 | tf_op jit(solution)/shard_map/all_to_all | solution.py:309
  46.7 2.2 %copy-done = bf16[16,512,256]{2,1,0:T(8,128)(2,1)S(1)} copy-done((bf16[16,512,256]{2,1,0:T(8,128)(2,1)S(1)}, bf16[16,512,256]{2,1,0:T(8,128)(2,1)}, u32[]{:S(2)}) %copy-start) | copy-done | bytes 4194328
  48.9 2.2 %copy-done.1 = bf16[16,512,256]{2,1,0:T(8,128)(2,1)S(1)} copy-done((bf16[16,512,256]{2,1,0:T(8,128)(2,1)S(1)}, bf16[16,512,256]{2,1,0:T(8,128)(2,1)}, u32[]{:S(2)}) %copy-start.1) | copy-done | bytes 4194328
  51.0 11.2 %shard_map.91.receivers = bf16[128,128,128]{2,1,0:T(8,128)(2,1)S(1)} custom-call(f32[64,4096]{1,0:T(8,128)} %bitcast.63, bf16[16,512,256]{2,1,0:T(8,128)(2,1)S(1)} %copy-done.1, bf16[16,512,256]{2,1,0:T(8,128)(2,1)S(1)} %copy-done, f32[2,128,128]{2,1,0:T(8,128)S(1)} %copy-done.2), custom_call_target="tpu_custom_call" | custom-call | flops 6000000000 | bytes 14680064 | tf_op jit(solution)/shard_map/pallas_call | solution.py:205
  62.2 1.9 %copy-done.5 = bf16[128,128,128]{2,1,0:T(8,128)(2,1)} copy-done((bf16[128,128,128]{2,1,0:T(8,128)(2,1)}, bf16[128,128,128]{2,1,0:T(8,128)(2,1)S(1)}, u32[]{:S(2)}) %copy-start.5) | copy-done | bytes 4194328
  64.2 7.4 %all-to-all-done.4 = f32[16,8,4096]{2,1,0:T(8,128)S(1)} async-done(((f32[16,8,4096]{2,1,0:T(8,128)}), f32[16,8,4096]{2,1,0:T(8,128)S(1)}, u32[]{:S(2)}, u32[]{:S(2)}) %all-to-all-start.4) | async-done | bytes 2097184 | tf_op jit(solution)/shard_map/all_to_all | solution.py:309
  71.5 13.7 %shard_map.92 = f32[1024,128]{1,0:T(8,128)S(1)} custom-call(f32[128,4096]{1,0:T(8,128)S(1)} %bitcast.60, bf16[16,512,256]{2,1,0:T(8,128)(2,1)} %constant.328.clone.th_ref.high, bf16[16,512,256]{2,1,0:T(8,128)(2,1)} %constant.329.clone.tl_ref.low, bf16[128,128,128]{2,1,0:T(8,128)(2,1)} %copy-done.5, s32[64,128]{1,0:T(8,128)S(1)} %fusion.15.bins_ref, ...), custom_call_target="tpu_custom_call" | custom-call | flops 8999999488 | bytes 16777216 | tf_op jit(solution)/shard_map/pallas_call | solution.py:144
  85.4 6.2 %collective-permute-start = (f32[128,640]{1,0:T(8,128)S(1)}, f32[128,640]{1,0:T(8,128)S(1)}, u32[]{:S(2)}, u32[]{:S(2)}) collective-permute-start(f32[128,640]{1,0:T(8,128)S(1)} %pad_maximum_fusion), channel_id=1, source_target_pairs={{0,1},{1,0},{2,3},{3,2},{4,5},{5,4},{6,7},{7,6},{8,9},{9,8},{10,11... | collective-permute-start | bytes 983048 | tf_op jit(solution)/shard_map/ppermute | solution.py:320
  91.6 1.2 %collective-permute-done = f32[128,640]{1,0:T(8,128)S(1)} collective-permute-done((f32[128,640]{1,0:T(8,128)S(1)}, f32[128,640]{1,0:T(8,128)S(1)}, u32[]{:S(2)}, u32[]{:S(2)}) %collective-permute-start) | collective-permute-done | bytes 327712 | tf_op jit(solution)/shard_map/ppermute | solution.py:320
  93.1 21.0 %all_to_all.47 = f32[128,1,640]{2,1,0:T(1,128)S(1)} all-to-all(f32[128,1,640]{2,1,0:T(1,128)S(1)} %all_to_all.37), channel_id=1, replica_groups=mesh['x'=4,'z'=8,'y'=4,'core'=2] {'x','z','y'}, dimensions={0} | all-to-all | bytes 655360 | tf_op jit(solution)/shard_map/all_to_all | solution.py:321
  114.4 0.7 bitcast_divide_fusion
  (52 shorter events, 6.4 us)
Async XLA Ops:
  1.3 12.8 %copy-start.7 = (s32[64,128]{1,0:T(8,128)S(1)}, s32[64,128]{1,0:T(8,128)}, u32[]{:S(2)}) copy-start(s32[64,128]{1,0:T(8,128)} %param.13) | copy-start | bytes 98308
  1.3 13.2 %copy-start.8 = (s32[1024]{0:T(1024)S(1)}, s32[1024]{0:T(1024)}, u32[]{:S(2)}) copy-start(s32[1024]{0:T(1024)} %param.14) | copy-start | bytes 12292
  3.1 37.7 %copy-start.6 = (f32[8,8,2,2048]{3,1,2,0:T(8,128)}, f32[8,8,2,2048]{3,1,2,0:T(8,128)S(1)}, u32[]{:S(2)}) copy-start(f32[8,8,2,2048]{3,1,2,0:T(8,128)S(1)} %copy.30) | copy-start | bytes 3145732
  6.5 15.0 %all-to-all-start.2 = ((f32[16,1,4096]{2,1,0:T(1,128)}), f32[16,1,4096]{2,1,0:T(1,128)S(1)}, u32[]{:S(2)}, u32[]{:S(2)}) async-start(f32[16,1,4096]{2,1,0:T(1,128)} %bitcast.8), calls=%async_computation.2 | async-start | bytes 524288 | tf_op jit(solution)/shard_map/all_to_all | solution.py:267
  22.7 17.7 %all-to-all-start.3 = ((f32[8,2,4096]{2,1,0:T(2,128)}), f32[8,2,4096]{2,1,0:T(2,128)S(1)}, u32[]{:S(2)}, u32[]{:S(2)}) async-start(f32[8,2,4096]{2,1,0:T(2,128)} %broadcast_in_dim.155), calls=%async_computation.3 | async-start | bytes 524288 | tf_op jit(solution)/shard_map/all_to_all | solution.py:278
  41.0 5.6 %copy-start.2 = (f32[2,128,128]{2,1,0:T(8,128)S(1)}, f32[2,128,128]{2,1,0:T(8,128)}, u32[]{:S(2)}) copy-start(f32[2,128,128]{2,1,0:T(8,128)} %constant.332.clone.gain_ref) | copy-start | bytes 393220
  42.8 28.8 %all-to-all-start.4 = ((f32[16,8,4096]{2,1,0:T(8,128)}), f32[16,8,4096]{2,1,0:T(8,128)S(1)}, u32[]{:S(2)}, u32[]{:S(2)}) async-start(f32[16,8,4096]{2,1,0:T(8,128)} %broadcast_in_dim.162), calls=%async_computation.4 | async-start | bytes 4194304 | tf_op jit(solution)/shard_map/all_to_all | solution.py:309
  46.7 2.2 %copy-start = (bf16[16,512,256]{2,1,0:T(8,128)(2,1)S(1)}, bf16[16,512,256]{2,1,0:T(8,128)(2,1)}, u32[]{:S(2)}) copy-start(bf16[16,512,256]{2,1,0:T(8,128)(2,1)} %constant.329.clone.tl_ref.low) | copy-start | bytes 12582916
  48.9 2.2 %copy-start.1 = (bf16[16,512,256]{2,1,0:T(8,128)(2,1)S(1)}, bf16[16,512,256]{2,1,0:T(8,128)(2,1)}, u32[]{:S(2)}) copy-start(bf16[16,512,256]{2,1,0:T(8,128)(2,1)} %constant.328.clone.th_ref.high) | copy-start | bytes 12582916
  51.0 20.5 %copy-start.3 = (bf16[256,128]{1,0:T(8,128)(2,1)S(1)}, bf16[256,128]{1,0:T(8,128)(2,1)}, u32[]{:S(2)}) copy-start(bf16[256,128]{1,0:T(8,128)(2,1)} %constant.331.clone.bl_ref) | copy-start | bytes 196612
  51.0 20.5 %copy-start.4 = (bf16[256,128]{1,0:T(8,128)(2,1)S(1)}, bf16[256,128]{1,0:T(8,128)(2,1)}, u32[]{:S(2)}) copy-start(bf16[256,128]{1,0:T(8,128)(2,1)} %constant.330.clone.bh_ref) | copy-start | bytes 196612
  62.2 1.9 %copy-start.5 = (bf16[128,128,128]{2,1,0:T(8,128)(2,1)}, bf16[128,128,128]{2,1,0:T(8,128)(2,1)S(1)}, u32[]{:S(2)}) copy-start(bf16[128,128,128]{2,1,0:T(8,128)(2,1)S(1)} %shard_map.91.receivers) | copy-start | bytes 12582916
  85.4 7.4 %collective-permute-start = (f32[128,640]{1,0:T(8,128)S(1)}, f32[128,640]{1,0:T(8,128)S(1)}, u32[]{:S(2)}, u32[]{:S(2)}) collective-permute-start(f32[128,640]{1,0:T(8,128)S(1)} %pad_maximum_fusion), channel_id=1, source_target_pairs={{0,1},{1,0},{2,3},{3,2},{4,5},{5,4},{6,7},{7,6},{8,9},{9,8},{10,11... | collective-permute-start | bytes 983048 | tf_op jit(solution)/shard_map/ppermute | solution.py:320
